TPU v7x, 128 devices: a whole 4x4x4 slice. The times are simulated.
128 devices in a mesh: blk: 32 (over x, z, y_lo), dp: 4 (over y_hi, core).
Axes of the slice: x: 4, y: 4 (y_hi: 2, y_lo: 2; y = y_hi * 2 + y_lo), z: 4, core: 2. Of those that a mesh axis runs over, the one named last changes fastest.
Arguments:
- embeddings: bfloat16 [32768, 512], P(('dp', 'blk')), may hold values from -16 to 16
- centers: bfloat16 [65536, 512], P(('blk', 'dp')), may hold values from -10 to 10
- labels: int32 [32768], P(('dp', 'blk')), may hold values from 0 to 65535
Outputs:
- loss: float32 [32768], P(('dp', 'blk'))
All inputs are finite; a program needn't handle non-finite values.
Results may differ from a plain program's by a relative error of at most 0.0017.
Values may be sent and summed in bfloat16 or wider, within the bound.
No kernel may reach another device: no remote copies, remote signals or barrier semaphores. Data moves between devices by JAX's collectives and lax.ppermute only.
A program may use at most 128 MiB of HBM per device.

v0:
```python
import math
import jax
import jax.numpy as jnp
from jax import lax
from jax.sharding import Mesh
from jax.sharding import PartitionSpec as P

BLK = ("blk_0", "blk_1", "blk_2")
DP_BLK = ("dp", "blk_0", "blk_1", "blk_2")
BLK_DP = ("blk_0", "blk_1", "blk_2", "dp")
EPSILON = 1e-06
LOGIT_SCALE = 30.0
MARGIN = 0.5


def laid_out(tiles, dim):
    lengths = list(tiles.shape[1:])
    lengths[dim] *= tiles.shape[0]
    return jnp.moveaxis(tiles, 0, dim).reshape(lengths)


def sent_to_all(x, axis):
    length = lax.axis_size(axis)
    return lax.all_to_all(jnp.broadcast_to(x[None], (length, *x.shape)), axis, 0, 0, tiled=True)


def collect(x, axis, dim):
    return laid_out(sent_to_all(x, axis), dim)


def gather_in_order(x, axes, order):
    tiles = x[None]
    for k in order:
        tiles = lax.all_gather(tiles, axes[k], axis=0, tiled=True)
    carried = [lax.axis_size(axes[k]) for k in reversed(order)]
    tiles = tiles.reshape(*carried, *x.shape)
    turned = sorted(range(len(order)), key=lambda place: order[len(order) - 1 - place])
    return tiles.transpose(*turned, *range(len(order), tiles.ndim)).reshape(-1, *x.shape)


def gather_axes(x, axes, order, dim):
    return laid_out(gather_in_order(x, axes, order), dim)


def split_up(x, dim, length):
    before, after = (x.shape[:dim], x.shape[dim + 1 :])
    return jnp.moveaxis(x.reshape(*before, length, -1, *after), dim, 0)


def sum_at_owner(x, axis, dim):
    length = lax.axis_size(axis)
    tiles = lax.all_to_all(split_up(x, dim, length), axis, 0, 0, tiled=True)
    return jnp.sum(tiles, axis=0)


def unit_rows(matrix):
    values = matrix.astype(jnp.float32)
    return (values * lax.rsqrt(jnp.sum(values * values, axis=1, keepdims=True) + EPSILON)).astype(
        jnp.bfloat16
    )


def margin_loss(other_sum, target_cos):
    sine = jnp.sqrt(jnp.maximum(1.0 - target_cos * target_cos, 0.0))
    shifted = target_cos * math.cos(MARGIN) - sine * math.sin(MARGIN)
    return (
        LOGIT_SCALE
        + jnp.log(other_sum + jnp.exp(LOGIT_SCALE * shifted - LOGIT_SCALE))
        - LOGIT_SCALE * shifted
    )


def block_terms(rows, row_labels, centers_block, class_start):
    cosine = jnp.einsum("nd,cd->nc", rows, centers_block, preferred_element_type=jnp.float32)
    columns = class_start + jnp.arange(centers_block.shape[0], dtype=jnp.int32)
    is_target = row_labels[:, None] == columns[None, :]
    other_sum = jnp.sum(
        jnp.where(is_target, 0.0, jnp.exp(LOGIT_SCALE * cosine - LOGIT_SCALE)), axis=1
    )
    target_cos = jnp.sum(jnp.where(is_target, cosine, 0.0), axis=1)
    return (other_sum, target_cos)


def body(embeddings, centers, labels):
    emb_unit = unit_rows(embeddings)
    center_unit = unit_rows(centers)
    shard_classes = center_unit.shape[0]
    group_count = lax.axis_size("dp")
    group_index = lax.axis_index("dp")
    group_rows, group_labels = (collect(emb_unit, "dp", 0), collect(labels, "dp", 0))
    group_total = group_rows.shape[0]
    zeros_sum = jnp.zeros((group_total,), jnp.float32)
    pieces = gather_axes(center_unit, BLK, (2, 0, 1), 0)
    span_rows = math.gcd(math.gcd(pieces.shape[0], shard_classes), 512)

    def one_span(accum, step_index):
        first = step_index * span_rows
        block_rows = lax.dynamic_slice_in_dim(pieces, step_index * span_rows, span_rows, 0)
        class_start = (
            first // shard_classes * group_count + group_index
        ) * shard_classes + first % shard_classes
        other_part, target_part = block_terms(group_rows, group_labels, block_rows, class_start)
        return ((accum[0] + other_part, accum[1] + target_part), None)

    result, ignored = lax.scan(
        one_span, (zeros_sum, zeros_sum), jnp.arange(pieces.shape[0] // span_rows, dtype=jnp.int32)
    )
    other_group, target_group = result
    other_sum, target_cos = (
        sum_at_owner(other_group, "dp", 0),
        sum_at_owner(target_group, "dp", 0),
    )
    return margin_loss(other_sum, target_cos)


def solution(mesh):
    finer = Mesh(mesh.devices.reshape(4, 4, 2, mesh.shape["dp"]), ("blk_0", "blk_1", "blk_2", "dp"))
    placed = (P(DP_BLK, None), P(BLK_DP, None), P(DP_BLK))
    return jax.shard_map(body, mesh=finer, in_specs=placed, out_specs=P(DP_BLK), check_vma=False)
```

profile of v0, /device:TPU:1, one launch (start us, length us, event | category | flops | bytes accessed | tf_op | source)
XLA Modules:
  0.0 432.8 jit_solution(17319401200410657807)
XLA Ops:
  9.8 27.1 %all-gather.9.cloned.1.call-done = bf16[1024,512]{1,0:T(8,128)(2,1)} async-done(((bf16[512,512]{1,0:T(8,128)(2,1)}), bf16[1024,512]{1,0:T(8,128)(2,1)}) %all-gather.9.cloned.1.call-update) | async-done | bytes 1048592 | tf_op jit(solution)/shard_map/all_gather | solution.py:34
  37.1 50.8 %all-gather.5.cloned.1.call-done = bf16[8,512,512]{2,1,0:T(8,128)(2,1)} async-done(((bf16[2,512,512]{2,1,0:T(8,128)(2,1)}), bf16[8,512,512]{2,1,0:T(8,128)(2,1)}) %all-gather.5.cloned.1.call-update) | async-done | bytes 4194320 | tf_op jit(solution)/shard_map/all_gather | solution.py:34
  89.2 5.0 %all-to-all-start = ((s32[4,1,256]{2,1,0:T(1,128)}), s32[4,1,256]{2,1,0:T(1,128)S(1)}, u32[]{:S(2)}, u32[]{:S(2)}) async-start(s32[4,1,256]{2,1,0:T(1,128)} %broadcast_in_dim.31), calls=%async_computation | async-start | bytes 8192 | tf_op jit(solution)/shard_map/all_to_all | solution.py:24
  94.4 4.3 %all-to-all-done = s32[4,1,256]{2,1,0:T(1,128)S(1)} async-done(((s32[4,1,256]{2,1,0:T(1,128)}), s32[4,1,256]{2,1,0:T(1,128)S(1)}, u32[]{:S(2)}, u32[]{:S(2)}) %all-to-all-start) | async-done | bytes 4128 | tf_op jit(solution)/shard_map/all_to_all | solution.py:24
  99.8 4.2 all-to-all-start.1
  104.0 140.1 %all-gather.7.cloned.1.call-done = bf16[32,512,512]{2,1,0:T(8,128)(2,1)} async-done(((bf16[8,512,512]{2,1,0:T(8,128)(2,1)}), bf16[32,512,512]{2,1,0:T(8,128)(2,1)}) %all-gather.7.cloned.1.call-update) | async-done | bytes 16777232 | tf_op jit(solution)/shard_map/all_gather | solution.py:34
  244.1 13.7 %copy.7 = bf16[4,4,2,512,512]{4,3,2,1,0:T(8,128)(2,1)} copy(bf16[4,4,2,512,512]{4,3,2,0,1:T(8,128)(2,1)} %bitcast.35) | data formatting | bytes 33554432 | tf_op jit(solution)/shard_map/transpose | solution.py:38
  257.9 150.0 %while.15 = (s32[]{:T(128)}, f32[1024]{0:T(1024)S(1)}, f32[1024]{0:T(1024)}, s32[4,256]{1,0:T(4,128)S(1)}, s32[32]{0:T(128)S(1)}, /*index=5*/s32[]{:T(128)}, bf1...) while((s32[]{:T(128)}, f32[1024]{0:T(1024)S(1)}, ...), condition=%wide.region_5.6_spmd.clone, body=%wide.region_2.5_spmd.clone.sunk | while | flops 540543488 | bytes 1622475 | solution.py:105
  259.2 2.1 fusion.15
  263.2 2.1 fusion.15
  267.9 2.1 fusion.15
  272.6 2.1 fusion.15
  277.3 2.1 fusion.15
  282.0 2.1 fusion.15
  286.7 2.1 fusion.15
  291.5 2.1 fusion.15
  296.2 2.1 fusion.15
  305.6 2.1 fusion.15
  315.0 2.1 fusion.15
  324.4 2.1 fusion.15
  333.8 2.1 fusion.15
  343.2 2.1 fusion.15
  352.7 2.1 fusion.15
  362.1 2.1 fusion.15
  366.8 2.1 fusion.15
  371.5 2.1 fusion.15
  380.9 2.1 fusion.15
  390.3 2.1 fusion.15
  399.7 2.1 fusion.15
  407.8 9.3 %all_to_all.32 = f32[4,1,256]{2,1,0:T(1,128)S(1)} all-to-all(f32[4,1,256]{2,1,0:T(1,128)S(1)} %bitcast.38), channel_id=1, replica_groups=mesh['blk_0'=4,'blk_1'=4,'blk_2'=2,'dp'=4] {'dp'}, dimensions={0} | all-to-all | bytes 8192 | tf_op jit(solution)/shard_map/all_to_all | solution.py:52
  417.2 3.9 all-to-all-start.3
  421.0 4.6 %all-to-all-done.3 = f32[4,1,256]{2,1,0:T(1,128)S(1)} async-done(((f32[4,1,256]{2,1,0:T(1,128)}), f32[4,1,256]{2,1,0:T(1,128)S(1)}, u32[]{:S(2)}, u32[]{:S(2)}) %all-to-all-start.3) | async-done | bytes 4128 | tf_op jit(solution)/shard_map/all_to_all | solution.py:52
  (165 shorter events, 89.5 us)
Async XLA Ops:
  6.5 30.5 %all-gather.9.cloned.1.call-start = ((), (), s32[]{:S(2)}) async-start(), calls=%async_computation.6 | async-start | bytes 1572864 | tf_op jit(solution)/shard_map/all_gather | solution.py:34
  9.8 78.1 %all-gather.5.cloned.1.call-start = ((), (), s32[]{:S(2)}) async-start(), calls=%async_computation.4 | async-start | bytes 5242880 | tf_op jit(solution)/shard_map/all_gather | solution.py:34
  37.0 207.1 %all-gather.7.cloned.1.call-start = ((), (), s32[]{:S(2)}) async-start(), calls=%async_computation.5 | async-start | bytes 20971520 | tf_op jit(solution)/shard_map/all_gather | solution.py:34
  87.9 0.7 copy-start.1
  87.9 6.2 %copy-start = (bf16[256,512]{1,0:T(8,128)(2,1)S(1)}, bf16[256,512]{1,0:T(8,128)(2,1)}, u32[]{:S(2)}) copy-start(bf16[256,512]{1,0:T(8,128)(2,1)} %param.5) | copy-start | bytes 786436
  89.2 9.5 %all-to-all-start = ((s32[4,1,256]{2,1,0:T(1,128)}), s32[4,1,256]{2,1,0:T(1,128)S(1)}, u32[]{:S(2)}, u32[]{:S(2)}) async-start(s32[4,1,256]{2,1,0:T(1,128)} %broadcast_in_dim.31), calls=%async_computation | async-start | bytes 8192 | tf_op jit(solution)/shard_map/all_to_all | solution.py:24
  99.8 158.1 %all-to-all-start.1 = ((bf16[4,256,512]{2,1,0:T(8,128)(2,1)}), bf16[4,256,512]{2,1,0:T(8,128)(2,1)S(1)}, u32[]{:S(2)}, u32[]{:S(2)}) async-start(bf16[4,256,512]{2,1,0:T(8,128)(2,1)} %broadcast_in_dim.33), calls=%async_computation.1 | async-start | bytes 2097152 | tf_op jit(solution)/shard_map/all_to_all | solution.py:24
  417.2 8.4 %all-to-all-start.3 = ((f32[4,1,256]{2,1,0:T(1,128)}), f32[4,1,256]{2,1,0:T(1,128)S(1)}, u32[]{:S(2)}, u32[]{:S(2)}) async-start(f32[4,1,256]{2,1,0:T(1,128)} %bitcast.6), calls=%async_computation.3 | async-start | bytes 8192 | tf_op jit(solution)/shard_map/all_to_all | solution.py:52
Sparse Core Ops, SparseCore 0:
  9.9 27.0 all-gather.8
  38.7 49.1 all-gather.4
  89.6 154.4 all-gather.6
where the time goes:
time: 436 us; the launch traced here: 433 us
  waiting for transfers between devices  227 us (52%)
  matrix products  67.3 us (15%)
  other arithmetic  44.4 us (10%)
  local copies, waits for them, and re-layouts  35.7 us (8%)
  loops' own time  22.9 us (5%)
  starting transfers between devices  13.1 us (3%)
  between operations  13.1 us (3%)
  blocking collectives  9.34 us (2%)
    all_gather x3, waiting for transfers between devices, gather_in_order(): tiles = lax.all_gather(tiles, axes[k], axis=0, tiled=True)  218 us
    dot_general x32, matrix products, block_terms(): jnp.einsum('nd,cd->nc', rows, centers_block, preferred_element_type=jnp.f...  67.3 us
    add x32, other arithmetic, one_span(): return ((accum[0] + other_part, accum[1] + target_part), None)  40.1 us
    another operation x1, loops' own time, body(): lax.scan(one_span, (zeros_sum, zeros_sum), jnp.arange(pieces.shape[0] //...  22.9 us
    dynamic_slice x32, local copies, waits for them, and re-layouts, body(): lax.scan(one_span, (zeros_sum, zeros_sum), jnp.arange(pieces.shape[0] //...  19.5 us
    transpose x1, local copies, waits for them, and re-layouts, gather_in_order(): tiles.transpose(*turned, *range(len(order), tiles.ndim))  13.7 us
    all_to_all x1, blocking collectives, sum_at_owner(): tiles = lax.all_to_all(split_up(x, dim, length), axis, 0, 0, tiled=True)  9.34 us
    all_to_all x2, starting transfers between devices, sent_to_all(): lax.all_to_all(jnp.broadcast_to(x[None], (length, *x.shape)), axis, 0, 0,...  9.18 us
  transfers between devices with their start and end apart: 6, of which 5 were waited for; matrix products, arithmetic and copies ran while one was open for 4% of the time, Pallas kernels for 0%

commit v1 on v0

--- a/solution.py
+++ b/solution.py
@@ -31,7 +31,10 @@
 def gather_in_order(x, axes, order):
     tiles = x[None]
     for k in order:
-        tiles = lax.all_gather(tiles, axes[k], axis=0, tiled=True)
+        size = lax.axis_size(axes[k])
+        blocks = jnp.stack([tiles for _ in range(size)])
+        blocks = lax.all_to_all(blocks, axes[k], split_axis=0, concat_axis=0)
+        tiles = jnp.concatenate(blocks, axis=0)
     carried = [lax.axis_size(axes[k]) for k in reversed(order)]
     tiles = tiles.reshape(*carried, *x.shape)
     turned = sorted(range(len(order)), key=lambda place: order[len(order) - 1 - place])

time: 436 us -> 463 us (1.062)
  blocking collectives: 9.34 us -> 74.1 us
  waiting for transfers between devices: 227 us -> 190 us
  between operations: 13.1 us -> 0.07 us
  starting transfers between devices: 13.1 us -> 23.9 us
  local copies, waits for them, and re-layouts: 35.7 us -> 40.9 us
    all_gather x3 -> x0, waiting for transfers between devices: 218 us -> none  [gather_in_order(): tiles = lax.all_gather(tiles, axes[k], axis=0, tiled=True)]
    all_to_all x0 -> x1, waiting for transfers between devices: none -> 182 us  [gather_in_order(): blocks = lax.all_to_all(blocks, axes[k], split_axis=0, concat_axis=0)]
    all_to_all x0 -> x2, blocking collectives: none -> 66.2 us  [gather_in_order(): blocks = lax.all_to_all(blocks, axes[k], split_axis=0, concat_axis=0)]
    all_to_all x0 -> x1, starting transfers between devices: none -> 7.09 us  [gather_in_order(): blocks = lax.all_to_all(blocks, axes[k], split_axis=0, concat_axis=0)]
    another operation x0 -> x2, local copies, waits for them, and re-layouts: none -> 6.18 us  [gather_in_order(): blocks = jnp.stack([tiles for _ in range(size)])]
  transfers between devices with their start and end apart: 6 -> 4, of which waited for: 5 -> 4; matrix products, arithmetic and copies ran while one was open for 4% -> 4% of each run, Pallas kernels for 0% -> 0%
where the time goes in v1:
time: 463 us; the launch traced here: 460 us
  waiting for transfers between devices  190 us (41%)
  blocking collectives  74.1 us (16%)
  matrix products  67.2 us (15%)
  other arithmetic  43.5 us (9%)
  local copies, waits for them, and re-layouts  40.9 us (9%)
  starting transfers between devices  23.9 us (5%)
  loops' own time  20.5 us (4%)
    all_to_all x1, waiting for transfers between devices, gather_in_order(): blocks = lax.all_to_all(blocks, axes[k], split_axis=0, concat_axis=0)  182 us
    dot_general x32, matrix products, block_terms(): jnp.einsum('nd,cd->nc', rows, centers_block, preferred_element_type=jnp.f...  67.2 us
    all_to_all x2, blocking collectives, gather_in_order(): blocks = lax.all_to_all(blocks, axes[k], split_axis=0, concat_axis=0)  66.2 us
    add x32, other arithmetic, one_span(): return ((accum[0] + other_part, accum[1] + target_part), None)  39.9 us
    another operation x1, loops' own time, body(): lax.scan(one_span, (zeros_sum, zeros_sum), jnp.arange(pieces.shape[0] //...  20.5 us
    dynamic_slice x32, local copies, waits for them, and re-layouts, body(): lax.scan(one_span, (zeros_sum, zeros_sum), jnp.arange(pieces.shape[0] //...  18.5 us
    transpose x1, local copies, waits for them, and re-layouts, gather_in_order(): tiles.transpose(*turned, *range(len(order), tiles.ndim))  13.8 us
    all_to_all x2, starting transfers between devices, sent_to_all(): lax.all_to_all(jnp.broadcast_to(x[None], (length, *x.shape)), axis, 0, 0,...  13 us
  transfers between devices with their start and end apart: 4, of which 4 were waited for; matrix products, arithmetic and copies ran while one was open for 4% of the time, Pallas kernels for 0%

profile of v1, /device:TPU:1, one launch (start us, length us, event | category | flops | bytes accessed | tf_op | source)
XLA Modules:
  0.0 459.7 jit_solution(13390531870832766287)
XLA Ops:
  1.3 6.0 %all-to-all-start = ((s32[4,1,256]{2,1,0:T(1,128)}), s32[4,1,256]{2,1,0:T(1,128)S(1)}, u32[]{:S(2)}, u32[]{:S(2)}) async-start(s32[4,1,256]{2,1,0:T(1,128)} %broadcast_in_dim.28), calls=%async_computation | async-start | bytes 8192 | tf_op jit(solution)/shard_map/all_to_all | solution.py:24
  11.8 15.4 %all_to_all.47 = bf16[2,1,512,512]{3,2,1,0:T(8,128)(2,1)S(1)} all-to-all(bf16[2,1,512,512]{3,2,1,0:T(8,128)(2,1)S(1)} %pad_maximum_fusion), channel_id=1, replica_groups=mesh['blk_0'=4,'blk_1'=4,'blk_2'=2,'dp'=4] {'blk_2'}, dimensions={0} | all-to-all | bytes 2097152 | tf_op jit(solution)/shard_map/all_to_all | solution.py:36
  27.6 50.8 %all_to_all.48 = bf16[4,2,512,512]{3,2,1,0:T(8,128)(2,1)S(1)} all-to-all(bf16[4,2,512,512]{3,2,1,0:T(8,128)(2,1)S(1)} %stack.10), channel_id=1, replica_groups=mesh['blk_0'=4,'blk_1'=4,'blk_2'=2,'dp'=4] {'blk_0'}, dimensions={0} | all-to-all | bytes 8388608 | tf_op jit(solution)/shard_map/all_to_all | solution.py:36
  78.4 5.8 %stack.11 = bf16[4,8,512,512]{3,2,1,0:T(8,128)(2,1)} broadcast(bf16[8,512,512]{2,1,0:T(8,128)(2,1)S(1)} %bitcast.37), dimensions={1,2,3} | broadcast | bytes 20971520 | tf_op jit(solution)/shard_map/stack | solution.py:35
  84.2 7.1 %all-to-all-start.3 = ((bf16[4,8,512,512]{3,2,1,0:T(8,128)(2,1)}), bf16[4,8,512,512]{3,2,1,0:T(8,128)(2,1)}, u32[]{:S(2)}, u32[]{:S(2)}) async-start(bf16[4,8,512,512]{3,2,1,0:T(8,128)(2,1)} %stack.11), calls=%async_computation.3 | async-start | bytes 33554432 | tf_op jit(solution)/shard_map/all_to_all | solution.py:36
  91.6 181.7 %all-to-all-done.3 = bf16[4,8,512,512]{3,2,1,0:T(8,128)(2,1)} async-done(((bf16[4,8,512,512]{3,2,1,0:T(8,128)(2,1)}), bf16[4,8,512,512]{3,2,1,0:T(8,128)(2,1)}, u32[]{:S(2)}, u32[]{:S(2)}) %all-to-all-start.3) | async-done | bytes 16777248 | tf_op jit(solution)/shard_map/all_to_all | solution.py:36
  274.3 7.0 %all-to-all-start.4 = ((bf16[4,256,512]{2,1,0:T(8,128)(2,1)}), bf16[4,256,512]{2,1,0:T(8,128)(2,1)S(1)}, u32[]{:S(2)}, u32[]{:S(2)}) async-start(bf16[4,256,512]{2,1,0:T(8,128)(2,1)} %broadcast_in_dim.29), calls=%async_computation.4 | async-start | bytes 2097152 | tf_op jit(solution)/shard_map/all_to_all | solution.py:24
  281.3 13.8 %copy.7 = bf16[4,4,2,512,512]{4,3,2,1,0:T(8,128)(2,1)} copy(bf16[4,4,2,512,512]{4,3,2,0,1:T(8,128)(2,1)} %bitcast.4) | data formatting | bytes 33554432 | tf_op jit(solution)/shard_map/transpose | solution.py:41
  296.4 146.3 %while.15 = (s32[]{:T(128)}, f32[1024]{0:T(1024)S(1)}, f32[1024]{0:T(1024)}, s32[4,256]{1,0:T(4,128)S(1)}, s32[32]{0:T(128)S(1)}, /*index=5*/s32[]{:T(128)}, bf1...) while((s32[]{:T(128)}, f32[1024]{0:T(1024)S(1)}, ...), condition=%wide.region_5.6_spmd.clone, body=%wide.region_2.5_spmd.clone.sunk | while | flops 540543488 | bytes 1622475 | solution.py:108
  297.6 2.1 fusion.16
  301.6 2.1 fusion.16
  306.2 2.1 fusion.16
  310.8 2.1 fusion.16
  315.4 2.1 fusion.16
  319.9 2.1 fusion.16
  329.1 2.1 fusion.16
  333.7 2.1 fusion.16
  338.3 2.1 fusion.16
  347.5 2.1 fusion.16
  356.7 2.1 fusion.16
  365.9 2.1 fusion.16
  375.1 2.1 fusion.16
  384.3 2.1 fusion.16
  393.4 2.1 fusion.16
  402.6 2.1 fusion.16
  411.8 2.1 fusion.16
  421.0 2.1 fusion.16
  430.2 2.1 fusion.16
  439.4 2.1 fusion.16
  442.8 7.9 %all_to_all.49 = f32[4,1,256]{2,1,0:T(1,128)S(1)} all-to-all(f32[4,1,256]{2,1,0:T(1,128)S(1)} %bitcast.41), channel_id=1, replica_groups=mesh['blk_0'=4,'blk_1'=4,'blk_2'=2,'dp'=4] {'dp'}, dimensions={0} | all-to-all | bytes 8192 | tf_op jit(solution)/shard_map/all_to_all | solution.py:55
  450.6 3.9 all-to-all-start.6
  454.5 4.6 all-to-all-done.6
  (161 shorter events, 93.3 us)
Async XLA Ops:
  1.3 10.6 %all-to-all-start = ((s32[4,1,256]{2,1,0:T(1,128)}), s32[4,1,256]{2,1,0:T(1,128)S(1)}, u32[]{:S(2)}, u32[]{:S(2)}) async-start(s32[4,1,256]{2,1,0:T(1,128)} %broadcast_in_dim.28), calls=%async_computation | async-start | bytes 8192 | tf_op jit(solution)/shard_map/all_to_all | solution.py:24
  84.2 7.1 %copy-start = (bf16[256,512]{1,0:T(8,128)(2,1)S(1)}, bf16[256,512]{1,0:T(8,128)(2,1)}, u32[]{:S(2)}) copy-start(bf16[256,512]{1,0:T(8,128)(2,1)} %param.5) | copy-start | bytes 786436
  84.2 189.0 %all-to-all-start.3 = ((bf16[4,8,512,512]{3,2,1,0:T(8,128)(2,1)}), bf16[4,8,512,512]{3,2,1,0:T(8,128)(2,1)}, u32[]{:S(2)}, u32[]{:S(2)}) async-start(bf16[4,8,512,512]{3,2,1,0:T(8,128)(2,1)} %stack.11), calls=%async_computation.3 | async-start | bytes 33554432 | tf_op jit(solution)/shard_map/all_to_all | solution.py:36
  274.3 22.1 %all-to-all-start.4 = ((bf16[4,256,512]{2,1,0:T(8,128)(2,1)}), bf16[4,256,512]{2,1,0:T(8,128)(2,1)S(1)}, u32[]{:S(2)}, u32[]{:S(2)}) async-start(bf16[4,256,512]{2,1,0:T(8,128)(2,1)} %broadcast_in_dim.29), calls=%async_computation.4 | async-start | bytes 2097152 | tf_op jit(solution)/shard_map/all_to_all | solution.py:24
  450.6 8.5 %all-to-all-start.6 = ((f32[4,1,256]{2,1,0:T(1,128)}), f32[4,1,256]{2,1,0:T(1,128)S(1)}, u32[]{:S(2)}, u32[]{:S(2)}) async-start(f32[4,1,256]{2,1,0:T(1,128)} %bitcast.8), calls=%async_computation.6 | async-start | bytes 8192 | tf_op jit(solution)/shard_map/all_to_all | solution.py:55
